TPU v7x, 32 devices: a whole 2x2x4 slice. The times are simulated.
32 devices in a mesh: groups: 2 (over x), blk: 16 (over z, y, core).
Axes of the slice: x: 2, y: 2, z: 4, core: 2. Of those that a mesh axis runs over, the one named last changes fastest.
Arguments:
- queries: float32 [64, 8192], P(('groups', 'blk')), parts along dimension 0, may hold values from -50 to 50
- prefix_keys: float32 [4096, 512], P(('groups', 'blk')), parts along dimension 0, may hold values from -40 to 40
- prefix_values: float32 [4096, 512], P(('groups', 'blk')), parts along dimension 0, may hold values from -8 to 8
- out_weight: float32 [8192, 4096], P('blk'), may hold values from -0.0625 to 0.0625
- lengths: int32 [4], P('groups'), parts along dimension 0, may hold values from 512 to 2048, as said below
Outputs:
- mixed: float32 [64, 4096], P(('groups', 'blk')), parts along dimension 0
There are 2 independent parts, one for each index of `groups`. A program takes and returns all parts, laid end to end along the dimension named above; an argument that names none is the same for every part. Nothing has to cross between parts.
Inputs may be any that keep to these rules, and one draw needn't show every extreme that they name: `lengths`: each request sees at least the first 512 prefix tokens, and some request sees all 2048 of them.
All inputs are finite; a program needn't handle non-finite values.
Results may differ from a plain program's by a relative error of at most 0.0003.
Values sent between devices are 32-bit elements; how exact they have to be, the bound alone decides.
A program may use at most 128 MiB of HBM per device.

v0:
```python
import math

import jax
import jax.numpy as jnp
from jax import lax
from jax.sharding import PartitionSpec as P

H = 64
KVH = 4
HD = 128
REQ_TOK = 16


HIGHEST = lax.Precision.HIGHEST
NEG_FILL = -1e30


def head_partials(query_rows, first_row, keys_split, values_split, key_pos, lengths):
    row_count = query_rows.shape[0]
    kv_count = keys_split.shape[1]
    head_count = query_rows.shape[1] // HD
    grouped = query_rows.reshape(row_count, kv_count, head_count // kv_count, HD)
    scores = jnp.einsum(
        "tgje,pge->tgjp", grouped, keys_split, precision=HIGHEST, preferred_element_type=jnp.float32
    ) * (1.0 / math.sqrt(HD))
    request_ids = (first_row + jnp.arange(row_count, dtype=jnp.int32)) // REQ_TOK
    request_table = jnp.arange(lengths.shape[0], dtype=jnp.int32)
    limits = jnp.sum(
        jnp.where(request_ids[:, None] == request_table[None, :], lengths[None, :], 0), axis=1
    )
    visible = key_pos[None, :] < limits[:, None]
    visible_four = visible[:, None, None, :]
    masked = jnp.where(visible_four, scores, NEG_FILL)
    peak_vals = jnp.max(masked, axis=3)
    weights = jnp.where(visible_four, jnp.exp(masked - peak_vals[..., None]), 0.0)
    totals = jnp.sum(weights, axis=3)
    mixed_values = jnp.einsum(
        "tgjp,pge->tgje",
        weights,
        values_split,
        precision=HIGHEST,
        preferred_element_type=jnp.float32,
    )
    return (
        mixed_values.reshape(row_count, head_count * HD),
        peak_vals.reshape(row_count, head_count),
        totals.reshape(row_count, head_count),
    )


def visit_blocks(running, shard_rows, first_row, keys_split, values_split, key_pos, lengths):
    row_count = shard_rows.shape[0]
    step_rows = 32

    def advance(step_id, current):
        row_begin = first_row + step_id * step_rows
        rows_now = lax.dynamic_slice_in_dim(shard_rows, step_id * step_rows, step_rows, 0)
        parts_now = head_partials(rows_now, row_begin, keys_split, values_split, key_pos, lengths)
        return tuple(
            (
                lax.dynamic_update_slice_in_dim(whole_arr, piece_now, row_begin, 0)
                for whole_arr, piece_now in zip(current, parts_now)
            )
        )

    return lax.fori_loop(0, row_count // step_rows, advance, running)


def per_device(queries, prefix_keys, prefix_values, out_weight, lengths):
    blocks = lax.axis_size("blk")
    position = lax.axis_index("blk")
    local_rows = queries.shape[0]
    total_rows = local_rows * blocks
    feature_count = H * HD
    key_count = prefix_keys.shape[0]
    group_size = H // KVH
    sub_count = blocks // KVH
    sub_len = key_count // sub_count
    key_send = (
        prefix_keys.reshape(sub_count, sub_len, KVH, HD)
        .transpose(0, 2, 1, 3)
        .reshape(blocks, sub_len, HD)
    )
    value_send = (
        prefix_values.reshape(sub_count, sub_len, KVH, HD)
        .transpose(0, 2, 1, 3)
        .reshape(blocks, sub_len, HD)
    )
    held_keys, held_values = (
        lax.all_to_all(key_send, "blk", split_axis=0, concat_axis=0, tiled=True),
        lax.all_to_all(value_send, "blk", split_axis=0, concat_axis=0, tiled=True),
    )
    sub_index = position // KVH
    source_ids = jnp.arange(blocks, dtype=jnp.int32)
    held_pos = (
        source_ids[:, None] * key_count
        + sub_index * sub_len
        + jnp.arange(sub_len, dtype=jnp.int32)[None, :]
    ).reshape(blocks * sub_len)
    held_keys = held_keys.reshape(blocks * sub_len, 1, HD)
    held_values = held_values.reshape(blocks * sub_len, 1, HD)
    query_heads = queries.reshape(local_rows, KVH, group_size * HD).transpose(1, 0, 2)
    query_send = jnp.broadcast_to(
        query_heads[None], (sub_count, KVH, local_rows, group_size * HD)
    ).reshape(blocks, local_rows, group_size * HD)
    query_held = lax.all_to_all(query_send, "blk", split_axis=0, concat_axis=0, tiled=True).reshape(
        total_rows, group_size * HD
    )
    empty_heads = (
        jnp.zeros((total_rows, group_size * HD), jnp.float32),
        jnp.zeros((total_rows, group_size), jnp.float32),
        jnp.zeros((total_rows, group_size), jnp.float32),
    )
    part_sums, part_peaks, part_totals = visit_blocks(
        empty_heads, query_held, 0, held_keys, held_values, held_pos, lengths
    )
    back_sums, back_peaks, back_totals = (
        lax.all_to_all(part_sums, "blk", split_axis=0, concat_axis=0, tiled=True),
        lax.all_to_all(part_peaks, "blk", split_axis=0, concat_axis=0, tiled=True),
        lax.all_to_all(part_totals, "blk", split_axis=0, concat_axis=0, tiled=True),
    )
    sums_split = back_sums.reshape(sub_count, KVH, local_rows, group_size, HD)
    peaks_split = back_peaks.reshape(sub_count, KVH, local_rows, group_size)
    overall = jnp.max(peaks_split, axis=0)
    factor = jnp.exp(peaks_split - overall[None])
    numerator = jnp.sum(sums_split * factor[..., None], axis=0)
    denominator = jnp.sum(
        back_totals.reshape(sub_count, KVH, local_rows, group_size) * factor, axis=0
    )
    attended = (
        (numerator / denominator[..., None])
        .transpose(1, 0, 2, 3)
        .reshape(local_rows, feature_count)
    )
    feature_rows = lax.all_to_all(attended, "blk", split_axis=1, concat_axis=0, tiled=True)
    return lax.psum_scatter(
        jnp.dot(feature_rows, out_weight, precision=HIGHEST, preferred_element_type=jnp.float32),
        "blk",
        scatter_dimension=0,
        tiled=True,
    )


def solution(mesh):
    in_specs = (
        P(("groups", "blk"), None),
        P(("groups", "blk"), None),
        P(("groups", "blk"), None),
        P("blk", None),
        P("groups"),
    )
    out_specs = P(("groups", "blk"), None)
    return jax.shard_map(
        per_device, mesh=mesh, in_specs=in_specs, out_specs=out_specs, check_vma=False
    )
```

profile of v0, /device:TPU:0, one launch (start us, length us, event | category | flops | bytes accessed | tf_op | source)
XLA Modules:
  0.0 200.5 jit_solution(15443193091474331846)
XLA Ops:
  6.5 0.9 reshape.156
  7.5 0.8 broadcast_in_dim.66
  8.3 7.4 %all-to-all-start.1 = ((f32[16,2,2048]{2,1,0:T(2,128)}), f32[16,2,2048]{2,1,0:T(2,128)S(1)}, u32[]{:S(2)}, u32[]{:S(2)}) async-start(f32[16,2,2048]{2,1,0:T(2,128)} %bitcast.5), calls=%async_computation.1 | async-start | bytes 524288 | tf_op jit(solution)/shard_map/all_to_all | solution.py:106
  15.7 1.0 reshape.153
  17.5 8.3 %all-to-all-done.1 = f32[16,2,2048]{2,1,0:T(2,128)S(1)} async-done(((f32[16,2,2048]{2,1,0:T(2,128)}), f32[16,2,2048]{2,1,0:T(2,128)S(1)}, u32[]{:S(2)}, u32[]{:S(2)}) %all-to-all-start.1) | async-done | bytes 262176 | tf_op jit(solution)/shard_map/all_to_all | solution.py:106
  25.7 3.5 %all-to-all-start = ((f32[16,32,128]{2,1,0:T(8,128)}), f32[16,32,128]{2,1,0:T(8,128)S(1)}, u32[]{:S(2)}, u32[]{:S(2)}) async-start(f32[16,32,128]{2,1,0:T(8,128)} %bitcast.1), calls=%async_computation | async-start | bytes 524288 | tf_op jit(solution)/shard_map/all_to_all | solution.py:90
  29.4 1.0 reshape.160
  31.2 0.7 fusion.8
  32.0 7.3 %all-to-all-done = f32[16,32,128]{2,1,0:T(8,128)S(1)} async-done(((f32[16,32,128]{2,1,0:T(8,128)}), f32[16,32,128]{2,1,0:T(8,128)S(1)}, u32[]{:S(2)}, u32[]{:S(2)}) %all-to-all-start) | async-done | bytes 262176 | tf_op jit(solution)/shard_map/all_to_all | solution.py:90
  39.3 3.5 %all-to-all-start.2 = ((f32[16,32,128]{2,1,0:T(8,128)}), f32[16,32,128]{2,1,0:T(8,128)S(1)}, u32[]{:S(2)}, u32[]{:S(2)}) async-start(f32[16,32,128]{2,1,0:T(8,128)} %bitcast.10), calls=%async_computation.2 | async-start | bytes 524288 | tf_op jit(solution)/shard_map/all_to_all | solution.py:91
  43.1 1.1 fusion.10
  45.3 7.5 %all-to-all-done.2 = f32[16,32,128]{2,1,0:T(8,128)S(1)} async-done(((f32[16,32,128]{2,1,0:T(8,128)}), f32[16,32,128]{2,1,0:T(8,128)S(1)}, u32[]{:S(2)}, u32[]{:S(2)}) %all-to-all-start.2) | async-done | bytes 262176 | tf_op jit(solution)/shard_map/all_to_all | solution.py:91
  52.8 3.5 %all-to-all-start.5 = ((f32[16,2,16]{2,1,0:T(2,128)}), f32[16,2,16]{2,1,0:T(2,128)S(1)}, u32[]{:S(2)}, u32[]{:S(2)}) async-start(f32[16,2,16]{2,1,0:T(2,128)} %bitcast.19), calls=%async_computation.5 | async-start | bytes 32768 | tf_op jit(solution)/shard_map/all_to_all | solution.py:120
  57.0 5.8 %all-to-all-done.5 = f32[16,2,16]{2,1,0:T(2,128)S(1)} async-done(((f32[16,2,16]{2,1,0:T(2,128)}), f32[16,2,16]{2,1,0:T(2,128)S(1)}, u32[]{:S(2)}, u32[]{:S(2)}) %all-to-all-start.5) | async-done | bytes 2080 | tf_op jit(solution)/shard_map/all_to_all | solution.py:120
  62.8 3.5 %all-to-all-start.4 = ((f32[16,2,16]{2,1,0:T(2,128)}), f32[16,2,16]{2,1,0:T(2,128)S(1)}, u32[]{:S(2)}, u32[]{:S(2)}) async-start(f32[16,2,16]{2,1,0:T(2,128)} %bitcast.16), calls=%async_computation.4 | async-start | bytes 32768 | tf_op jit(solution)/shard_map/all_to_all | solution.py:119
  66.3 1.1 convolution_bitcast_fusion
  67.5 0.8 all_to_all.44
  68.4 4.4 %all-to-all-done.4 = f32[16,2,16]{2,1,0:T(2,128)S(1)} async-done(((f32[16,2,16]{2,1,0:T(2,128)}), f32[16,2,16]{2,1,0:T(2,128)S(1)}, u32[]{:S(2)}, u32[]{:S(2)}) %all-to-all-start.4) | async-done | bytes 2080 | tf_op jit(solution)/shard_map/all_to_all | solution.py:119
  72.7 3.5 %all-to-all-start.3 = ((f32[16,2,2048]{2,1,0:T(2,128)}), f32[16,2,2048]{2,1,0:T(2,128)S(1)}, u32[]{:S(2)}, u32[]{:S(2)}) async-start(f32[16,2,2048]{2,1,0:T(2,128)} %all_to_all.44), calls=%async_computation.3 | async-start | bytes 524288 | tf_op jit(solution)/shard_map/all_to_all | solution.py:118
  76.4 9.9 %all-to-all-done.3 = f32[16,2,2048]{2,1,0:T(2,128)S(1)} async-done(((f32[16,2,2048]{2,1,0:T(2,128)}), f32[16,2,2048]{2,1,0:T(2,128)S(1)}, u32[]{:S(2)}, u32[]{:S(2)}) %all-to-all-start.3) | async-done | bytes 262176 | tf_op jit(solution)/shard_map/all_to_all | solution.py:118
  86.8 9.7 %all_to_all.61 = f32[2,16,512]{2,0,1:T(2,128)S(1)} all-to-all(f32[2,16,512]{2,0,1:T(2,128)S(1)} %copy.43), channel_id=1, replica_groups=mesh['groups'=2,'blk'=16] {'blk'}, dimensions={1} | all-to-all | bytes 131072 | tf_op jit(solution)/shard_map/all_to_all | solution.py:135
  96.6 8.0 %fusion.11 = f32[32,4096]{1,0:T(8,128)} fusion(f32[32,512]{1,0:T(8,128)S(1)} %all_to_all.53, f32[512,4096]{1,0:T(8,128)} %param.8), kind=kOutput, calls=%fused_computation.27 | convolution fusion | flops 805306368 | bytes 8978432 | tf_op jit(solution)/shard_map/dot_general | solution.py:137
  105.8 86.3 %all-reduce.3.cloned.1.call-done = f32[32,4096]{1,0:T(8,128)} async-done(((f32[32,4096]{1,0:T(8,128)}), f32[32,4096]{1,0:T(8,128)}) %all-reduce.3.cloned.1.call-update) | async-done | bytes 524304
  192.1 1.5 constant_dynamic-slice_fusion
  (28 shorter events, 5.1 us)
Async XLA Ops:
  8.3 17.4 %all-to-all-start.1 = ((f32[16,2,2048]{2,1,0:T(2,128)}), f32[16,2,2048]{2,1,0:T(2,128)S(1)}, u32[]{:S(2)}, u32[]{:S(2)}) async-start(f32[16,2,2048]{2,1,0:T(2,128)} %bitcast.5), calls=%async_computation.1 | async-start | bytes 524288 | tf_op jit(solution)/shard_map/all_to_all | solution.py:106
  25.7 13.5 %all-to-all-start = ((f32[16,32,128]{2,1,0:T(8,128)}), f32[16,32,128]{2,1,0:T(8,128)S(1)}, u32[]{:S(2)}, u32[]{:S(2)}) async-start(f32[16,32,128]{2,1,0:T(8,128)} %bitcast.1), calls=%async_computation | async-start | bytes 524288 | tf_op jit(solution)/shard_map/all_to_all | solution.py:90
  39.3 13.5 %all-to-all-start.2 = ((f32[16,32,128]{2,1,0:T(8,128)}), f32[16,32,128]{2,1,0:T(8,128)S(1)}, u32[]{:S(2)}, u32[]{:S(2)}) async-start(f32[16,32,128]{2,1,0:T(8,128)} %bitcast.10), calls=%async_computation.2 | async-start | bytes 524288 | tf_op jit(solution)/shard_map/all_to_all | solution.py:91
  43.1 61.4 %copy-start = (u32[32]{0:T(128)S(1)}, u32[32]{0:T(128)}, u32[]{:S(2)}) copy-start(u32[32]{0:T(128)} %constant.68) | copy-start | bytes 388
  52.8 9.9 %all-to-all-start.5 = ((f32[16,2,16]{2,1,0:T(2,128)}), f32[16,2,16]{2,1,0:T(2,128)S(1)}, u32[]{:S(2)}, u32[]{:S(2)}) async-start(f32[16,2,16]{2,1,0:T(2,128)} %bitcast.19), calls=%async_computation.5 | async-start | bytes 32768 | tf_op jit(solution)/shard_map/all_to_all | solution.py:120
  62.8 10.0 %all-to-all-start.4 = ((f32[16,2,16]{2,1,0:T(2,128)}), f32[16,2,16]{2,1,0:T(2,128)S(1)}, u32[]{:S(2)}, u32[]{:S(2)}) async-start(f32[16,2,16]{2,1,0:T(2,128)} %bitcast.16), calls=%async_computation.4 | async-start | bytes 32768 | tf_op jit(solution)/shard_map/all_to_all | solution.py:119
  72.7 13.5 %all-to-all-start.3 = ((f32[16,2,2048]{2,1,0:T(2,128)}), f32[16,2,2048]{2,1,0:T(2,128)S(1)}, u32[]{:S(2)}, u32[]{:S(2)}) async-start(f32[16,2,2048]{2,1,0:T(2,128)} %all_to_all.44), calls=%async_computation.3 | async-start | bytes 524288 | tf_op jit(solution)/shard_map/all_to_all | solution.py:118
  76.3 115.9 %all-reduce.3.cloned.1.call-start = ((), (), s32[]{:S(2)}) async-start(), calls=%async_computation.7 | async-start | bytes 1048576
Sparse Core Ops, SparseCore 0:
  104.7 87.4 all-reduce.2
where the time goes:
time: 201 us
  waiting for transfers between devices  130 us (65%)
  starting transfers between devices  25 us (12%)
  between operations  14.3 us (7%)
  local copies, waits for them, and re-layouts  10.4 us (5%)
  matrix products  10.2 us (5%)
  blocking collectives  9.67 us (5%)
    unnamed x2, waiting for transfers between devices  86.3 us
    all_to_all x1, waiting for transfers between devices, per_device(): lax.all_to_all(part_sums, 'blk', split_axis=0, concat_axis=0, tiled=True)  9.88 us
    all_to_all x1, blocking collectives, per_device(): lax.all_to_all(attended, 'blk', split_axis=1, concat_axis=0, tiled=True)  9.67 us
    all_to_all x1, waiting for transfers between devices, per_device(): lax.all_to_all(query_send, 'blk', split_axis=0, concat_axis=0, tiled=True)  8.27 us
    dot_general x1, matrix products, per_device(): jnp.dot(feature_rows, out_weight, precision=HIGHEST, preferred_element_ty...  7.98 us
    all_to_all x1, waiting for transfers between devices, per_device(): lax.all_to_all(value_send, 'blk', split_axis=0, concat_axis=0, tiled=True)  7.54 us
    all_to_all x1, starting transfers between devices, per_device(): lax.all_to_all(query_send, 'blk', split_axis=0, concat_axis=0, tiled=True)  7.39 us
    all_to_all x1, waiting for transfers between devices, per_device(): lax.all_to_all(key_send, 'blk', split_axis=0, concat_axis=0, tiled=True)  7.33 us
  transfers between devices with their start and end apart: 7, of which 7 were waited for; matrix products, arithmetic and copies ran while one was open for 5% of the time, Pallas kernels for 0%

commit v1 on v0

--- a/solution.py
+++ b/solution.py
@@ -1,8 +1,11 @@
+import functools
 import math
 
 import jax
 import jax.numpy as jnp
 from jax import lax
+from jax.experimental import pallas as pl
+from jax.experimental.pallas import tpu as pltpu
 from jax.sharding import PartitionSpec as P
 
 H = 64
@@ -140,6 +143,400 @@
         tiled=True,
     )
 
+def split_two(values):
+    high = values.astype(jnp.bfloat16)
+    return high, (values - high.astype(jnp.float32)).astype(jnp.bfloat16)
+
+
+def fused_kernel(
+    planes,
+    pieces,
+    weight_parts,
+    q_hbm,
+    k_hbm,
+    v_hbm,
+    w_hbm,
+    len_ref,
+    out_ref,
+    q_all,
+    q_rows,
+    k_all,
+    v_all,
+    scores,
+    w_full,
+    w_high,
+    w_low,
+    part_out,
+    part_in,
+    plane_out,
+    plane_in,
+    line_out,
+    line_in,
+    own_sem,
+    w_sem,
+    qz_send,
+    qz_recv,
+    qp_send,
+    qp_recv,
+    k_send,
+    k_recv,
+    v_send,
+    v_recv,
+    c_send,
+    c_recv,
+    r_send,
+    r_recv,
+    l_send,
+    l_recv,
+):
+    me = lax.axis_index("blk")
+    line = lax.div(me, planes)
+    spot = lax.rem(me, planes)
+    group_size = H // KVH
+    group_width = group_size * HD
+    local_rows = q_hbm.shape[0]
+    key_count = k_hbm.shape[0]
+    tile_rows = KVH * local_rows
+    row_total = planes * tile_rows
+    own_heads = group_size // planes
+    width = w_hbm.shape[1]
+
+    def remote(src, dst, send, recv, target):
+        return pltpu.make_async_remote_copy(
+            src_ref=src,
+            dst_ref=dst,
+            send_sem=send,
+            recv_sem=recv,
+            device_id={"blk": target},
+            device_id_type=pl.DeviceIdType.MESH,
+        )
+
+    def line_peer(step):
+        return lax.rem(line + step, KVH)
+
+    def plane_peer(step):
+        return lax.rem(spot + step, planes)
+
+    def head_cols(ref, head, size):
+        return ref.at[:, pl.ds(pl.multiple_of(head * size, size), size)]
+
+    line_steps = [2, 1, 3] if KVH == 4 else list(range(1, KVH))
+    plane_steps = list(range(1, planes))
+
+    own = [
+        pltpu.make_async_copy(head_cols(q_hbm, line, group_width), q_all.at[spot, 0], own_sem.at[0]),
+        pltpu.make_async_copy(head_cols(k_hbm, line, HD), k_all.at[0], own_sem.at[1]),
+        pltpu.make_async_copy(head_cols(v_hbm, line, HD), v_all.at[0], own_sem.at[2]),
+    ]
+    for copy in own:
+        copy.start()
+    w_step = w_hbm.shape[0] // weight_parts
+    w_copies = [
+        pltpu.make_async_copy(
+            w_hbm.at[pl.ds(n * w_step, w_step)], w_full.at[pl.ds(n * w_step, w_step)], w_sem.at[n]
+        )
+        for n in range(weight_parts)
+    ]
+    for copy in w_copies:
+        copy.start()
+
+    barrier = pltpu.get_barrier_semaphore()
+    for step in line_steps:
+        pl.semaphore_signal(
+            barrier,
+            inc=1,
+            device_id={"blk": line_peer(step) * planes + spot},
+            device_id_type=pl.DeviceIdType.MESH,
+        )
+    for step in plane_steps:
+        pl.semaphore_signal(
+            barrier,
+            inc=1,
+            device_id={"blk": line * planes + plane_peer(step)},
+            device_id_type=pl.DeviceIdType.MESH,
+        )
+    pl.semaphore_wait(barrier, len(line_steps) + len(plane_steps))
+
+    q_line, k_line, v_line = {}, {}, {}
+    for step in line_steps:
+        head = line_peer(step)
+        q_line[step] = remote(
+            head_cols(q_hbm, head, group_width),
+            q_all.at[spot, step],
+            qz_send.at[step],
+            qz_recv.at[step],
+            head * planes + spot,
+        )
+        q_line[step].start()
+    for source, target, send, recv, made in (
+        (k_hbm, k_all, k_send, k_recv, k_line),
+        (v_hbm, v_all, v_send, v_recv, v_line),
+    ):
+        for step in line_steps:
+            head = line_peer(step)
+            made[step] = remote(
+                head_cols(source, head, HD),
+                target.at[step],
+                send.at[step],
+                recv.at[step],
+                head * planes + spot,
+            )
+            made[step].start()
+
+    split_rows, split_cols = 16, width // 2
+
+    def split_part(part):
+        w_copies[part].wait()
+
+        def body(at, carry):
+            rows = pl.ds(pl.multiple_of(part * w_step + at * split_rows, split_rows), split_rows)
+            for half in range(width // split_cols):
+                cols = pl.ds(half * split_cols, split_cols)
+                high, low = split_two(w_full[rows, cols])
+                w_high[rows, cols] = high
+                w_low[rows, cols] = low
+            return carry
+
+        lax.fori_loop(0, w_step // split_rows, body, 0)
+
+    early = weight_parts // 2
+    for part in range(early):
+        split_part(part)
+
+    own[0].wait()
+    for step in line_steps:
+        q_line[step].wait_recv()
+    q_plane = {}
+    for step in plane_steps:
+        q_plane[step] = remote(
+            q_all.at[spot],
+            q_all.at[spot],
+            qp_send.at[step],
+            qp_recv.at[step],
+            line * planes + plane_peer(step),
+        )
+        q_plane[step].start()
+    for part in range(early, weight_parts):
+        split_part(part)
+    for step in plane_steps:
+        q_plane[step].wait_recv()
+
+    for place in range(planes):
+        for step in range(KVH):
+            first = place * tile_rows + step * local_rows
+            for head in range(group_size):
+                q_rows[pl.ds(head * row_total + first, local_rows), :] = q_all[
+                    place, step, :, pl.ds(head * HD, HD)
+                ]
+    query = q_rows[...]
+
+    columns = group_size * row_total
+    lane = lax.broadcasted_iota(jnp.int32, (1, columns), 1) % row_total
+    lane_line = (line - (lane % tile_rows) // local_rows + KVH) % KVH
+    token = (lane_line * planes + lane // tile_rows) * local_rows + lane % local_rows
+    request = token // REQ_TOK
+    limits = jnp.zeros((1, columns), jnp.int32)
+    for n in range(len_ref.shape[0]):
+        limits = jnp.where(request == n, len_ref[n], limits)
+
+    def key_place(step):
+        source = lax.rem(line - step + KVH, KVH) * planes + spot
+        return source * key_count + lax.broadcasted_iota(jnp.int32, (key_count, 1), 0)
+
+    scale = 1.0 / math.sqrt(HD)
+    peak = None
+    for step in [0] + line_steps:
+        if step == 0:
+            own[1].wait()
+        else:
+            k_line[step].wait_recv()
+        block = (
+            lax.dot_general(
+                k_all[step],
+                query,
+                (((1,), (1,)), ((), ())),
+                precision=HIGHEST,
+                preferred_element_type=jnp.float32,
+            )
+            * scale
+        )
+        block = jnp.where(key_place(step) < limits, block, NEG_FILL)
+        scores[step] = block
+        top = jnp.max(block, axis=0, keepdims=True)
+        peak = top if peak is None else jnp.maximum(peak, top)
+    total = jnp.zeros((1, columns), jnp.float32)
+    sums = jnp.zeros((HD, columns), jnp.float32)
+    for step in [0] + line_steps:
+        if step == 0:
+            own[2].wait()
+        else:
+            v_line[step].wait_recv()
+        weights = jnp.where(key_place(step) < limits, jnp.exp(scores[step] - peak), 0.0)
+        total = total + jnp.sum(weights, axis=0, keepdims=True)
+        sums = sums + lax.dot_general(
+            v_all[step],
+            weights,
+            (((0,), (0,)), ((), ())),
+            precision=HIGHEST,
+            preferred_element_type=jnp.float32,
+        )
+
+    part_cols = own_heads * row_total
+    for place in range(planes):
+        cols = slice(place * part_cols, (place + 1) * part_cols)
+        part_out[place, pl.ds(0, HD), :] = sums[:, cols]
+        part_out[place, pl.ds(HD, 1), :] = peak[:, cols]
+        part_out[place, pl.ds(HD + 1, 1), :] = total[:, cols]
+    combine = {}
+    for step in plane_steps:
+        place = plane_peer(step)
+        combine[step] = remote(
+            part_out.at[place],
+            part_in.at[step],
+            c_send.at[step],
+            c_recv.at[step],
+            line * planes + place,
+        )
+        combine[step].start()
+    for step in plane_steps:
+        combine[step].wait_recv()
+    peaks = [part_out[spot, pl.ds(HD, 1), :]] + [part_in[n, pl.ds(HD, 1), :] for n in plane_steps]
+    totals = [part_out[spot, pl.ds(HD + 1, 1), :]] + [
+        part_in[n, pl.ds(HD + 1, 1), :] for n in plane_steps
+    ]
+    overall = functools.reduce(jnp.maximum, peaks)
+    factors = [jnp.exp(value - overall) for value in peaks]
+    denominator = sum(value * factor for value, factor in zip(totals, factors))
+    numerator = part_out[spot, pl.ds(0, HD), :] * factors[0]
+    for step in plane_steps:
+        numerator = numerator + part_in[step, pl.ds(0, HD), :] * factors[step]
+    attended = (numerator / denominator).T
+    features = jnp.concatenate(
+        [attended[n * row_total : (n + 1) * row_total] for n in range(own_heads)], axis=1
+    )
+    high, low = split_two(features)
+    both = jnp.concatenate([high, low], axis=0)
+
+    piece = width // pieces
+    plane_copies = []
+    for n in range(pieces):
+        cols = pl.ds(n * piece, piece)
+        first = jnp.dot(both, w_high[:, cols], preferred_element_type=jnp.float32)
+        second = jnp.dot(high, w_low[:, cols], preferred_element_type=jnp.float32)
+        mixed = first[:row_total] + first[row_total:] + second
+        for place in range(planes):
+            plane_out[n, place] = mixed[place * tile_rows : (place + 1) * tile_rows]
+        made = {}
+        for step in plane_steps:
+            place = plane_peer(step)
+            made[step] = remote(
+                plane_out.at[n, place],
+                plane_in.at[n, step],
+                r_send.at[n, step],
+                r_recv.at[n, step],
+                line * planes + place,
+            )
+            made[step].start()
+        plane_copies.append(made)
+
+    line_copies = []
+    for n in range(pieces):
+        value = plane_out[n, spot]
+        for step in plane_steps:
+            plane_copies[n][step].wait_recv()
+            value = value + plane_in[n, step]
+        for step in range(KVH):
+            line_out[n, step] = value[step * local_rows : (step + 1) * local_rows]
+        made = {}
+        for step in line_steps:
+            target = lax.rem(line - step + KVH, KVH) * planes + spot
+            made[step] = remote(
+                line_out.at[n, step],
+                line_in.at[n, step],
+                l_send.at[n, step],
+                l_recv.at[n, step],
+                target,
+            )
+            made[step].start()
+        line_copies.append(made)
+    for n in range(pieces):
+        value = line_out[n, 0]
+        for step in line_steps:
+            line_copies[n][step].wait_recv()
+            value = value + line_in[n, step]
+        out_ref[:, pl.ds(n * piece, piece)] = value
+
+    for made in [q_line, k_line, v_line, q_plane, combine] + plane_copies + line_copies:
+        for copy in made.values():
+            copy.wait_send()
+
+
+def fused(queries, prefix_keys, prefix_values, out_weight, lengths):
+    blocks = lax.axis_size("blk")
+    planes = blocks // KVH
+    local_rows = queries.shape[0]
+    key_count = prefix_keys.shape[0]
+    depth, width = out_weight.shape
+    group_size = H // KVH
+    tile_rows = KVH * local_rows
+    row_total = planes * tile_rows
+    columns = group_size * row_total
+    part_cols = columns // planes
+    pieces, weight_parts = 4, 8
+    piece = width // pieces
+    f32 = jnp.float32
+    any_space = pl.BlockSpec(memory_space=pl.ANY)
+    sems = pltpu.SemaphoreType.DMA
+    return pl.pallas_call(
+        functools.partial(fused_kernel, planes, pieces, weight_parts),
+        out_shape=jax.ShapeDtypeStruct((local_rows, width), f32),
+        in_specs=[any_space] * 4 + [pl.BlockSpec(memory_space=pltpu.SMEM)],
+        out_specs=pl.BlockSpec(memory_space=pltpu.VMEM),
+        scratch_shapes=[
+            pltpu.VMEM((planes, KVH, local_rows, group_size * HD), f32),
+            pltpu.VMEM((columns, HD), f32),
+            pltpu.VMEM((KVH, key_count, HD), f32),
+            pltpu.VMEM((KVH, key_count, HD), f32),
+            pltpu.VMEM((KVH, key_count, columns), f32),
+            pltpu.VMEM((depth, width), f32),
+            pltpu.VMEM((depth, width), jnp.bfloat16),
+            pltpu.VMEM((depth, width), jnp.bfloat16),
+            pltpu.VMEM((planes, HD + 8, part_cols), f32),
+            pltpu.VMEM((planes, HD + 8, part_cols), f32),
+            pltpu.VMEM((pieces, planes, tile_rows, piece), f32),
+            pltpu.VMEM((pieces, planes, tile_rows, piece), f32),
+            pltpu.VMEM((pieces, KVH, local_rows, piece), f32),
+            pltpu.VMEM((pieces, KVH, local_rows, piece), f32),
+            sems((3,)),
+            sems((weight_parts,)),
+            sems((KVH,)),
+            sems((KVH,)),
+            sems((planes,)),
+            sems((planes,)),
+            sems((KVH,)),
+            sems((KVH,)),
+            sems((KVH,)),
+            sems((KVH,)),
+            sems((planes,)),
+            sems((planes,)),
+            sems((pieces, planes)),
+            sems((pieces, planes)),
+            sems((pieces, KVH)),
+            sems((pieces, KVH)),
+        ],
+        compiler_params=pltpu.CompilerParams(
+            collective_id=0, has_side_effects=True, vmem_limit_bytes=48 * 1024 * 1024
+        ),
+    )(queries, prefix_keys, prefix_values, out_weight, lengths)
+
+
+def fits(mesh):
+    blocks = mesh.shape["blk"]
+    if blocks % KVH or (H // KVH) % (blocks // KVH):
+        return False
+    planes = blocks // KVH
+    return planes > 1 and planes <= 8
+
 
 def solution(mesh):
     in_specs = (
@@ -151,5 +548,9 @@
     )
     out_specs = P(("groups", "blk"), None)
     return jax.shard_map(
-        per_device, mesh=mesh, in_specs=in_specs, out_specs=out_specs, check_vma=False
-    )
+        fused if fits(mesh) else per_device,
+        mesh=mesh,
+        in_specs=in_specs,
+        out_specs=out_specs,
+        check_vma=False,
+    )

time: 201 us -> 40.9 us (0.20)
  waiting for transfers between devices: 130 us -> 0 us
  Pallas kernels: 0 us -> 36.7 us
  starting transfers between devices: 25 us -> 0 us
  between operations: 14.3 us -> 0.01 us
  matrix products: 10.2 us -> 0 us
  blocking collectives: 9.67 us -> 0 us
  local copies, waits for them, and re-layouts: 10.4 us -> 4.01 us
    unnamed x2 -> x0, waiting for transfers between devices: 86.3 us -> none
    all_to_all x6 -> x0, waiting for transfers between devices: 43.2 us -> none  [the longest x1 9.88 us: per_device(): lax.all_to_all(part_sums, 'blk', split_axis=0, concat_axis=0, tiled=True)]
    pallas_call x0 -> x1, Pallas kernels: none -> 36.7 us  [fused(): pl.pallas_call(functools.partial(fused_kernel, planes, pieces, weight_par...]
    all_to_all x6 -> x0, starting transfers between devices: 25 us -> none  [the longest x1 7.39 us: per_device(): lax.all_to_all(query_send, 'blk', split_axis=0, concat_axis=0, tiled=True)]
    dot_general x3 -> x0, matrix products: 10.2 us -> none  [the longest x1 7.98 us: per_device(): jnp.dot(feature_rows, out_weight, precision=HIGHEST, preferred_element_ty...]
    all_to_all x1 -> x0, blocking collectives: 9.67 us -> none  [per_device(): lax.all_to_all(attended, 'blk', split_axis=1, concat_axis=0, tiled=True)]
    reshape x4 -> x0, local copies, waits for them, and re-layouts: 3.19 us -> none  [the longest x1 1.04 us: per_device(): prefix_keys.reshape(sub_count, sub_len, KVH, HD).transpose(0, 2, 1, 3)]
  transfers between devices with their start and end apart: 7 -> 0, of which waited for: 7 -> 0; matrix products, arithmetic and copies ran while one was open for 5% -> 0% of each run, Pallas kernels for 0% -> 0%
where the time goes in v1:
time: 40.9 us; the launch traced here: 40.7 us
  Pallas kernels  36.7 us (90%)
  local copies, waits for them, and re-layouts  4.01 us (10%)
    pallas_call x1, Pallas kernels, fused(): pl.pallas_call(functools.partial(fused_kernel, planes, pieces, weight_par...  36.7 us
    unnamed x9, local copies, waits for them, and re-layouts  4.01 us

profile of v1, /device:TPU:0, one launch (start us, length us, event | category | flops | bytes accessed | tf_op | source)
XLA Modules:
  0.0 40.7 jit_solution(10221929765511974537)
XLA Ops:
  0.0 0.0 copy-start
  0.0 0.9 %copy-done = f32[128,512]{1,0:T(8,128)S(1)} copy-done((f32[128,512]{1,0:T(8,128)S(1)}, f32[128,512]{1,0:T(8,128)}, u32[]{:S(2)}) %copy-start) | copy-done | bytes 262168
  1.0 0.0 copy-start.1
  1.0 0.9 %copy-done.1 = f32[128,512]{1,0:T(8,128)S(1)} copy-done((f32[128,512]{1,0:T(8,128)S(1)}, f32[128,512]{1,0:T(8,128)}, u32[]{:S(2)}) %copy-start.1) | copy-done | bytes 262168
  1.9 0.0 copy-start.2
  1.9 0.8 %copy-done.2 = f32[2,8192]{1,0:T(2,128)S(1)} copy-done((f32[2,8192]{1,0:T(2,128)S(1)}, f32[2,8192]{1,0:T(2,128)}, u32[]{:S(2)}) %copy-start.2) | copy-done | bytes 65560
  2.7 0.0 copy-start.3
  2.7 0.7 %copy-done.3 = s32[2]{0:T(128)S(1)} copy-done((s32[2]{0:T(128)S(1)}, s32[2]{0:T(128)}, u32[]{:S(2)}) %copy-start.3) | copy-done | bytes 32
  3.4 36.7 %shard_map.55 = f32[2,4096]{1,0:T(2,128)S(1)} custom-call(f32[2,8192]{1,0:T(2,128)S(1)} %copy-done.2, f32[128,512]{1,0:T(8,128)S(1)} %copy-done, f32[128,512]{1,0:T(8,128)S(1)} %copy-done.1, f32[512,4096]{1,0:T(8,128)} %w_hbm.1, s32[2]{0:T(128)S(1)} %copy-done.3), custom_call_target="tpu_custom_call" | custom-call | tf_op jit(solution)/shard_map/pallas_call | solution.py:490
  40.1 0.6 %copy.7 = f32[2,4096]{1,0:T(2,128)} copy(f32[2,4096]{1,0:T(2,128)S(1)} %shard_map.55) | data formatting | bytes 65536
Async XLA Ops:
  0.0 0.9 %copy-start = (f32[128,512]{1,0:T(8,128)S(1)}, f32[128,512]{1,0:T(8,128)}, u32[]{:S(2)}) copy-start(f32[128,512]{1,0:T(8,128)} %k_hbm.1) | copy-start | bytes 786436
  1.0 0.9 %copy-start.1 = (f32[128,512]{1,0:T(8,128)S(1)}, f32[128,512]{1,0:T(8,128)}, u32[]{:S(2)}) copy-start(f32[128,512]{1,0:T(8,128)} %v_hbm.1) | copy-start | bytes 786436
  1.9 0.8 %copy-start.2 = (f32[2,8192]{1,0:T(2,128)S(1)}, f32[2,8192]{1,0:T(2,128)}, u32[]{:S(2)}) copy-start(f32[2,8192]{1,0:T(2,128)} %q_hbm.1) | copy-start | bytes 196612
  2.7 0.7 %copy-start.3 = (s32[2]{0:T(128)S(1)}, s32[2]{0:T(128)}, u32[]{:S(2)}) copy-start(s32[2]{0:T(128)} %len_ref.1) | copy-start | bytes 28

commit v2 on v1

--- a/solution.py
+++ b/solution.py
@@ -156,8 +156,9 @@
     k_hbm,
     v_hbm,
     w_hbm,
+    len_hbm,
+    out_ref,
     len_ref,
-    out_ref,
     q_all,
     q_rows,
     k_all,
@@ -227,6 +228,7 @@
         pltpu.make_async_copy(head_cols(q_hbm, line, group_width), q_all.at[spot, 0], own_sem.at[0]),
         pltpu.make_async_copy(head_cols(k_hbm, line, HD), k_all.at[0], own_sem.at[1]),
         pltpu.make_async_copy(head_cols(v_hbm, line, HD), v_all.at[0], own_sem.at[2]),
+        pltpu.make_async_copy(len_hbm, len_ref, own_sem.at[3]),
     ]
     for copy in own:
         copy.start()
@@ -335,6 +337,7 @@
     lane_line = (line - (lane % tile_rows) // local_rows + KVH) % KVH
     token = (lane_line * planes + lane // tile_rows) * local_rows + lane % local_rows
     request = token // REQ_TOK
+    own[3].wait()
     limits = jnp.zeros((1, columns), jnp.int32)
     for n in range(len_ref.shape[0]):
         limits = jnp.where(request == n, len_ref[n], limits)
@@ -365,17 +368,19 @@
         top = jnp.max(block, axis=0, keepdims=True)
         peak = top if peak is None else jnp.maximum(peak, top)
     total = jnp.zeros((1, columns), jnp.float32)
+    for step in range(KVH):
+        weights = jnp.where(key_place(step) < limits, jnp.exp(scores[step] - peak), 0.0)
+        total = total + jnp.sum(weights, axis=0, keepdims=True)
+        scores[step] = weights
     sums = jnp.zeros((HD, columns), jnp.float32)
     for step in [0] + line_steps:
         if step == 0:
             own[2].wait()
         else:
             v_line[step].wait_recv()
-        weights = jnp.where(key_place(step) < limits, jnp.exp(scores[step] - peak), 0.0)
-        total = total + jnp.sum(weights, axis=0, keepdims=True)
         sums = sums + lax.dot_general(
             v_all[step],
-            weights,
+            scores[step],
             (((0,), (0,)), ((), ())),
             precision=HIGHEST,
             preferred_element_type=jnp.float32,
@@ -485,14 +490,15 @@
     pieces, weight_parts = 4, 8
     piece = width // pieces
     f32 = jnp.float32
-    any_space = pl.BlockSpec(memory_space=pl.ANY)
+    any_space = pl.BlockSpec(memory_space=pltpu.HBM)
     sems = pltpu.SemaphoreType.DMA
     return pl.pallas_call(
         functools.partial(fused_kernel, planes, pieces, weight_parts),
         out_shape=jax.ShapeDtypeStruct((local_rows, width), f32),
-        in_specs=[any_space] * 4 + [pl.BlockSpec(memory_space=pltpu.SMEM)],
+        in_specs=[any_space] * 5,
         out_specs=pl.BlockSpec(memory_space=pltpu.VMEM),
         scratch_shapes=[
+            pltpu.SMEM(lengths.shape, lengths.dtype),
             pltpu.VMEM((planes, KVH, local_rows, group_size * HD), f32),
             pltpu.VMEM((columns, HD), f32),
             pltpu.VMEM((KVH, key_count, HD), f32),
@@ -507,7 +513,7 @@
             pltpu.VMEM((pieces, planes, tile_rows, piece), f32),
             pltpu.VMEM((pieces, KVH, local_rows, piece), f32),
             pltpu.VMEM((pieces, KVH, local_rows, piece), f32),
-            sems((3,)),
+            sems((4,)),
             sems((weight_parts,)),
             sems((KVH,)),
             sems((KVH,)),
@@ -525,7 +531,7 @@
             sems((pieces, KVH)),
         ],
         compiler_params=pltpu.CompilerParams(
-            collective_id=0, has_side_effects=True, vmem_limit_bytes=48 * 1024 * 1024
+            collective_id=0, has_side_effects=True, vmem_limit_bytes=64 * 1024 * 1024
         ),
     )(queries, prefix_keys, prefix_values, out_weight, lengths)
 

time: 40.9 us -> 38.4 us (0.939)
  local copies, waits for them, and re-layouts: 4.01 us -> 1.38 us
    unnamed x9 -> x1, local copies, waits for them, and re-layouts: 4.01 us -> 1.38 us
where the time goes in v2:
time: 38.4 us; the launch traced here: 38.2 us
  Pallas kernels  36.9 us (96%)
  local copies, waits for them, and re-layouts  1.38 us (4%)
    pallas_call x1, Pallas kernels, fused(): pl.pallas_call(functools.partial(fused_kernel, planes, pieces, weight_par...  36.9 us
    unnamed x1, local copies, waits for them, and re-layouts  1.38 us

profile of v2, /device:TPU:0, one launch (start us, length us, event | category | flops | bytes accessed | tf_op | source)
XLA Modules:
  0.0 38.2 jit_solution(2404505839506869080)
XLA Ops:
  0.0 36.9 %shard_map.55 = f32[2,4096]{1,0:T(2,128)} custom-call(f32[2,8192]{1,0:T(2,128)} %q_hbm.1, f32[128,512]{1,0:T(8,128)} %k_hbm.1, f32[128,512]{1,0:T(8,128)} %v_hbm.1, f32[512,4096]{1,0:T(8,128)} %w_hbm.1, s32[2]{0:T(128)} %len_hbm.1), custom_call_target="tpu_custom_call" | custom-call | tf_op jit(solution)/shard_map/pallas_call | solution.py:495
  36.9 1.4 %copy.7 = f32[2,4096]{1,0:T(2,128)} copy(f32[2,4096]{1,0:T(2,128)} %shard_map.55) | data formatting | bytes 65536

commit v3 on v2

--- a/solution.py
+++ b/solution.py
@@ -12,6 +12,7 @@
 KVH = 4
 HD = 128
 REQ_TOK = 16
+PAIR = 2
 
 
 HIGHEST = lax.Precision.HIGHEST
@@ -170,6 +171,8 @@
     part_out,
     part_in,
     plane_out,
+    pair_in,
+    pair_out,
     plane_in,
     line_out,
     line_in,
@@ -185,6 +188,8 @@
     v_recv,
     c_send,
     c_recv,
+    p_send,
+    p_recv,
     r_send,
     r_recv,
     l_send,
@@ -193,6 +198,8 @@
     me = lax.axis_index("blk")
     line = lax.div(me, planes)
     spot = lax.rem(me, planes)
+    side, core = lax.div(spot, PAIR), lax.rem(spot, PAIR)
+    sides = planes // PAIR
     group_size = H // KVH
     group_width = group_size * HD
     local_rows = q_hbm.shape[0]
@@ -423,31 +430,59 @@
     both = jnp.concatenate([high, low], axis=0)
 
     piece = width // pieces
-    plane_copies = []
-    for n in range(pieces):
+    pair_copies, plane_copies, line_copies = [], [], []
+
+    def project(n):
         cols = pl.ds(n * piece, piece)
         first = jnp.dot(both, w_high[:, cols], preferred_element_type=jnp.float32)
         second = jnp.dot(high, w_low[:, cols], preferred_element_type=jnp.float32)
         mixed = first[:row_total] + first[row_total:] + second
         for place in range(planes):
-            plane_out[n, place] = mixed[place * tile_rows : (place + 1) * tile_rows]
+            plane_out[n, place % PAIR, place // PAIR] = mixed[
+                place * tile_rows : (place + 1) * tile_rows
+            ]
         made = {}
-        for step in plane_steps:
-            place = plane_peer(step)
+        for step in range(1, PAIR):
+            other = lax.rem(core + step, PAIR)
             made[step] = remote(
-                plane_out.at[n, place],
+                plane_out.at[n, other],
+                pair_in.at[n, step],
+                p_send.at[n, step],
+                p_recv.at[n, step],
+                line * planes + side * PAIR + other,
+            )
+            made[step].start()
+        pair_copies.append(made)
+
+    def add_pair(n):
+        value = plane_out[n, core]
+        for step in range(1, PAIR):
+            pair_copies[n][step].wait_recv()
+            value = value + pair_in[n, step]
+        pair_out[n] = value
+        made = {}
+        for step in range(1, sides):
+            other = lax.rem(side + step, sides)
+            made[step] = remote(
+                pair_out.at[n, other],
                 plane_in.at[n, step],
                 r_send.at[n, step],
                 r_recv.at[n, step],
-                line * planes + place,
+                line * planes + other * PAIR + core,
             )
             made[step].start()
         plane_copies.append(made)
 
-    line_copies = []
+    ahead = min(2, pieces)
+    for n in range(pieces + ahead):
+        if n < pieces:
+            project(n)
+        if n >= ahead:
+            add_pair(n - ahead)
+
     for n in range(pieces):
-        value = plane_out[n, spot]
-        for step in plane_steps:
+        value = pair_out[n, side]
+        for step in range(1, sides):
             plane_copies[n][step].wait_recv()
             value = value + plane_in[n, step]
         for step in range(KVH):
@@ -471,7 +506,7 @@
             value = value + line_in[n, step]
         out_ref[:, pl.ds(n * piece, piece)] = value
 
-    for made in [q_line, k_line, v_line, q_plane, combine] + plane_copies + line_copies:
+    for made in [q_line, k_line, v_line, q_plane, combine] + pair_copies + plane_copies + line_copies:
         for copy in made.values():
             copy.wait_send()
 
@@ -479,6 +514,7 @@
 def fused(queries, prefix_keys, prefix_values, out_weight, lengths):
     blocks = lax.axis_size("blk")
     planes = blocks // KVH
+    sides = planes // PAIR
     local_rows = queries.shape[0]
     key_count = prefix_keys.shape[0]
     depth, width = out_weight.shape
@@ -509,8 +545,10 @@
             pltpu.VMEM((depth, width), jnp.bfloat16),
             pltpu.VMEM((planes, HD + 8, part_cols), f32),
             pltpu.VMEM((planes, HD + 8, part_cols), f32),
-            pltpu.VMEM((pieces, planes, tile_rows, piece), f32),
-            pltpu.VMEM((pieces, planes, tile_rows, piece), f32),
+            pltpu.VMEM((pieces, PAIR, sides, tile_rows, piece), f32),
+            pltpu.VMEM((pieces, PAIR, sides, tile_rows, piece), f32),
+            pltpu.VMEM((pieces, sides, tile_rows, piece), f32),
+            pltpu.VMEM((pieces, sides, tile_rows, piece), f32),
             pltpu.VMEM((pieces, KVH, local_rows, piece), f32),
             pltpu.VMEM((pieces, KVH, local_rows, piece), f32),
             sems((4,)),
@@ -525,8 +563,10 @@
             sems((KVH,)),
             sems((planes,)),
             sems((planes,)),
-            sems((pieces, planes)),
-            sems((pieces, planes)),
+            sems((pieces, PAIR)),
+            sems((pieces, PAIR)),
+            sems((pieces, sides)),
+            sems((pieces, sides)),
             sems((pieces, KVH)),
             sems((pieces, KVH)),
         ],
@@ -541,7 +581,7 @@
     if blocks % KVH or (H // KVH) % (blocks // KVH):
         return False
     planes = blocks // KVH
-    return planes > 1 and planes <= 8
+    return planes % PAIR == 0 and planes <= 8
 
 
 def solution(mesh):

time: 38.4 us -> 37 us (0.964)
  Pallas kernels: 36.9 us -> 35.4 us
    pallas_call x1, Pallas kernels: 36.9 us -> 35.4 us  [fused(): pl.pallas_call(functools.partial(fused_kernel, planes, pieces, weight_par...]
where the time goes in v3:
time: 37 us; the launch traced here: 36.8 us
  Pallas kernels  35.4 us (96%)
  local copies, waits for them, and re-layouts  1.38 us (4%)
    pallas_call x1, Pallas kernels, fused(): pl.pallas_call(functools.partial(fused_kernel, planes, pieces, weight_par...  35.4 us
    unnamed x1, local copies, waits for them, and re-layouts  1.38 us

profile of v3, /device:TPU:0, one launch (start us, length us, event | category | flops | bytes accessed | tf_op | source)
XLA Modules:
  0.0 36.8 jit_solution(9772795723717134594)
XLA Ops:
  0.0 35.4 %shard_map.55 = f32[2,4096]{1,0:T(2,128)} custom-call(f32[2,8192]{1,0:T(2,128)} %q_hbm.1, f32[128,512]{1,0:T(8,128)} %k_hbm.1, f32[128,512]{1,0:T(8,128)} %v_hbm.1, f32[512,4096]{1,0:T(8,128)} %w_hbm.1, s32[2]{0:T(128)} %len_hbm.1), custom_call_target="tpu_custom_call" | custom-call | tf_op jit(solution)/shard_map/pallas_call | solution.py:531
  35.4 1.4 %copy.7 = f32[2,4096]{1,0:T(2,128)} copy(f32[2,4096]{1,0:T(2,128)} %shard_map.55) | data formatting | bytes 65536

commit v4 on v3

--- a/solution.py
+++ b/solution.py
@@ -175,7 +175,6 @@
     pair_out,
     plane_in,
     line_out,
-    line_in,
     own_sem,
     w_sem,
     qz_send,
@@ -194,6 +193,7 @@
     r_recv,
     l_send,
     l_recv,
+    o_sem,
 ):
     me = lax.axis_index("blk")
     line = lax.div(me, planes)
@@ -430,7 +430,7 @@
     both = jnp.concatenate([high, low], axis=0)
 
     piece = width // pieces
-    pair_copies, plane_copies, line_copies = [], [], []
+    pair_copies, plane_copies, line_copies, own_out = [], [], [], []
 
     def project(n):
         cols = pl.ds(n * piece, piece)
@@ -487,12 +487,18 @@
             value = value + plane_in[n, step]
         for step in range(KVH):
             line_out[n, step] = value[step * local_rows : (step + 1) * local_rows]
+        own_out.append(
+            pltpu.make_async_copy(
+                line_out.at[n, 0], out_ref.at[0, :, pl.ds(n * piece, piece)], o_sem.at[n]
+            )
+        )
+        own_out[n].start()
         made = {}
         for step in line_steps:
             target = lax.rem(line - step + KVH, KVH) * planes + spot
             made[step] = remote(
                 line_out.at[n, step],
-                line_in.at[n, step],
+                out_ref.at[step, :, pl.ds(n * piece, piece)],
                 l_send.at[n, step],
                 l_recv.at[n, step],
                 target,
@@ -500,11 +506,9 @@
             made[step].start()
         line_copies.append(made)
     for n in range(pieces):
-        value = line_out[n, 0]
+        own_out[n].wait()
         for step in line_steps:
             line_copies[n][step].wait_recv()
-            value = value + line_in[n, step]
-        out_ref[:, pl.ds(n * piece, piece)] = value
 
     for made in [q_line, k_line, v_line, q_plane, combine] + pair_copies + plane_copies + line_copies:
         for copy in made.values():
@@ -528,11 +532,11 @@
     f32 = jnp.float32
     any_space = pl.BlockSpec(memory_space=pltpu.HBM)
     sems = pltpu.SemaphoreType.DMA
-    return pl.pallas_call(
+    line_parts = pl.pallas_call(
         functools.partial(fused_kernel, planes, pieces, weight_parts),
-        out_shape=jax.ShapeDtypeStruct((local_rows, width), f32),
+        out_shape=jax.ShapeDtypeStruct((KVH, local_rows, width), f32),
         in_specs=[any_space] * 5,
-        out_specs=pl.BlockSpec(memory_space=pltpu.VMEM),
+        out_specs=any_space,
         scratch_shapes=[
             pltpu.SMEM(lengths.shape, lengths.dtype),
             pltpu.VMEM((planes, KVH, local_rows, group_size * HD), f32),
@@ -549,7 +553,6 @@
             pltpu.VMEM((pieces, PAIR, sides, tile_rows, piece), f32),
             pltpu.VMEM((pieces, sides, tile_rows, piece), f32),
             pltpu.VMEM((pieces, sides, tile_rows, piece), f32),
-            pltpu.VMEM((pieces, KVH, local_rows, piece), f32),
             pltpu.VMEM((pieces, KVH, local_rows, piece), f32),
             sems((4,)),
             sems((weight_parts,)),
@@ -569,11 +572,13 @@
             sems((pieces, sides)),
             sems((pieces, KVH)),
             sems((pieces, KVH)),
+            sems((pieces,)),
         ],
         compiler_params=pltpu.CompilerParams(
             collective_id=0, has_side_effects=True, vmem_limit_bytes=64 * 1024 * 1024
         ),
     )(queries, prefix_keys, prefix_values, out_weight, lengths)
+    return jnp.sum(line_parts, axis=0)
 
 
 def fits(mesh):

time: 37 us -> 36.7 us (level)
  other arithmetic: 0 us -> 1.58 us
  local copies, waits for them, and re-layouts: 1.38 us -> 0 us
  Pallas kernels: 35.4 us -> 35 us
    reduce_sum x0 -> x1, other arithmetic: none -> 1.58 us  [fused(): return jnp.sum(line_parts, axis=0)]
    unnamed x1 -> x0, local copies, waits for them, and re-layouts: 1.38 us -> none
    pallas_call x1, Pallas kernels: 35.4 us -> 35 us  [fused(): pl.pallas_call(functools.partial(fused_kernel, planes, pieces, weight_par...]
where the time goes in v4:
time: 36.7 us; the launch traced here: 36.6 us
  Pallas kernels  35 us (95%)
  other arithmetic  1.58 us (4%)
    pallas_call x1, Pallas kernels, fused(): pl.pallas_call(functools.partial(fused_kernel, planes, pieces, weight_par...  35 us
    reduce_sum x1, other arithmetic, fused(): return jnp.sum(line_parts, axis=0)  1.58 us

profile of v4, /device:TPU:0, one launch (start us, length us, event | category | flops | bytes accessed | tf_op | source)
XLA Modules:
  0.0 36.6 jit_solution(4133547160816756687)
XLA Ops:
  0.0 35.0 %shard_map.55 = f32[4,2,4096]{2,1,0:T(2,128)} custom-call(f32[2,8192]{1,0:T(2,128)} %q_hbm.1, f32[128,512]{1,0:T(8,128)} %k_hbm.1, f32[128,512]{1,0:T(8,128)} %v_hbm.1, f32[512,4096]{1,0:T(8,128)} %w_hbm.1, s32[2]{0:T(128)} %len_hbm.1), custom_call_target="tpu_custom_call" | custom-call | tf_op jit(solution)/shard_map/pallas_call | solution.py:535
  35.0 1.6 %reduce_sum.9 = f32[2,4096]{1,0:T(2,128)} reduce(f32[4,2,4096]{2,1,0:T(2,128)} %shard_map.55, f32[]{:T(128)} %constant.0.clone.1), dimensions={0}, to_apply=%region_0.0 | reduce | flops 24576 | bytes 163844 | tf_op jit(solution)/shard_map/reduce_sum | solution.py:581

commit v5 on v4

--- a/solution.py
+++ b/solution.py
@@ -228,9 +228,24 @@
     def head_cols(ref, head, size):
         return ref.at[:, pl.ds(pl.multiple_of(head * size, size), size)]
 
-    line_steps = [2, 1, 3] if KVH == 4 else list(range(1, KVH))
+    line_steps = [1, 3, 2] if KVH == 4 else list(range(1, KVH))
     plane_steps = list(range(1, planes))
 
+    barrier = pltpu.get_barrier_semaphore()
+    for step in line_steps:
+        pl.semaphore_signal(
+            barrier,
+            inc=1,
+            device_id={"blk": line_peer(step) * planes + spot},
+            device_id_type=pl.DeviceIdType.MESH,
+        )
+    for step in plane_steps:
+        pl.semaphore_signal(
+            barrier,
+            inc=1,
+            device_id={"blk": line * planes + plane_peer(step)},
+            device_id_type=pl.DeviceIdType.MESH,
+        )
     own = [
         pltpu.make_async_copy(head_cols(q_hbm, line, group_width), q_all.at[spot, 0], own_sem.at[0]),
         pltpu.make_async_copy(head_cols(k_hbm, line, HD), k_all.at[0], own_sem.at[1]),
@@ -246,24 +261,6 @@
         )
         for n in range(weight_parts)
     ]
-    for copy in w_copies:
-        copy.start()
-
-    barrier = pltpu.get_barrier_semaphore()
-    for step in line_steps:
-        pl.semaphore_signal(
-            barrier,
-            inc=1,
-            device_id={"blk": line_peer(step) * planes + spot},
-            device_id_type=pl.DeviceIdType.MESH,
-        )
-    for step in plane_steps:
-        pl.semaphore_signal(
-            barrier,
-            inc=1,
-            device_id={"blk": line * planes + plane_peer(step)},
-            device_id_type=pl.DeviceIdType.MESH,
-        )
     pl.semaphore_wait(barrier, len(line_steps) + len(plane_steps))
 
     q_line, k_line, v_line = {}, {}, {}
@@ -291,6 +288,9 @@
                 head * planes + spot,
             )
             made[step].start()
+
+    for copy in w_copies:
+        copy.start()
 
     split_rows, split_cols = 16, width // 2
 

time: 36.7 us -> 36.5 us (level)
  no operation moved by 1% of the time
where the time goes in v5:
time: 36.5 us; the launch traced here: 36.4 us
  Pallas kernels  34.8 us (95%)
  other arithmetic  1.58 us (4%)
    pallas_call x1, Pallas kernels, fused(): pl.pallas_call(functools.partial(fused_kernel, planes, pieces, weight_par...  34.8 us
    reduce_sum x1, other arithmetic, fused(): return jnp.sum(line_parts, axis=0)  1.58 us

profile of v5, /device:TPU:0, one launch (start us, length us, event | category | flops | bytes accessed | tf_op | source)
XLA Modules:
  0.0 36.4 jit_solution(395335186994438047)
XLA Ops:
  0.0 34.8 %shard_map.55 = f32[4,2,4096]{2,1,0:T(2,128)} custom-call(f32[2,8192]{1,0:T(2,128)} %q_hbm.1, f32[128,512]{1,0:T(8,128)} %k_hbm.1, f32[128,512]{1,0:T(8,128)} %v_hbm.1, f32[512,4096]{1,0:T(8,128)} %w_hbm.1, s32[2]{0:T(128)} %len_hbm.1), custom_call_target="tpu_custom_call" | custom-call | tf_op jit(solution)/shard_map/pallas_call | solution.py:535
  34.8 1.6 %reduce_sum.9 = f32[2,4096]{1,0:T(2,128)} reduce(f32[4,2,4096]{2,1,0:T(2,128)} %shard_map.55, f32[]{:T(128)} %constant.0.clone.1), dimensions={0}, to_apply=%region_0.0 | reduce | flops 24576 | bytes 163844 | tf_op jit(solution)/shard_map/reduce_sum | solution.py:581
